TPU v7x, 256 devices: a whole 4x4x8 slice. The times are simulated.
256 devices in a mesh: dp: 4 (over x), wide: 64 (over y, z, core).
Axes of the slice: x: 4, y: 4, z: 8, core: 2. Of those that a mesh axis runs over, the one named last changes fastest.
Arguments:
- clips: bfloat16 [4, 64, 4, 128, 512], P('dp', 'wide'), may hold values from -8 to 8
- w_spatial: bfloat16 [4608, 512], P(None, 'dp'), may hold values from -0.09375 to 0.09375
- w_time: bfloat16 [1536, 512], replicated, may hold values from -0.15625 to 0.15625
- norm_gain: float32 [512], replicated, may hold values from 0.1 to 1.9
- norm_bias: float32 [512], replicated, may hold values from -0.6 to 0.6
- grad_out: bfloat16 [4, 64, 512, 512], P('dp', None, 'wide'), may hold values from -16 to 16
Outputs:
- grad_clips: bfloat16 [4, 64, 4, 128, 512], P('dp', 'wide')
- spatial_grad: float32 [4608, 512], P('dp', 'wide')
- time_grad: float32 [1536, 512], P('dp', 'wide')
All inputs are finite; a program needn't handle non-finite values.
Results may differ from a plain program's by a relative error of at most 0.009.
Values may be sent and summed in bfloat16 or wider, within the bound.
A program may use at most 128 MiB of HBM per device.

v0:
```python
import jax
import jax.numpy as jnp
from jax import lax
from jax.sharding import PartitionSpec as P

G = 32
FRAMES = 8


EPSILON = 1e-06
CONTRACT_ROWS = (((0,), (0,)), ((), ()))
CONTRACT_COLS = (((1,), (1,)), ((), ()))


def pad_frames(frames):
    return jnp.pad(frames, ((0, 0), (1, 1), (1, 1), (0, 0)))


def spatial_forward(frames, weights):
    frame_total, row_count, col_count, chan_count = frames.shape
    padded = pad_frames(frames)
    accum_out = jnp.zeros((frame_total * row_count * col_count, weights.shape[1]), jnp.float32)
    for tap_index in range(9):
        row_off, col_off = (tap_index // 3, tap_index % 3)
        window = padded[:, row_off : row_off + row_count, col_off : col_off + col_count, :].reshape(
            -1, chan_count
        )
        tap_weight = weights[tap_index * chan_count : (tap_index + 1) * chan_count]
        accum_out = accum_out + jnp.dot(window, tap_weight, preferred_element_type=jnp.float32)
    return accum_out.reshape(frame_total, row_count, col_count, -1)


def spatial_backward(frames, grad_hidden, weights):
    frame_total, row_count, col_count, chan_count = frames.shape
    padded_in = pad_frames(frames)
    padded_grad = pad_frames(grad_hidden)
    grad_flat = grad_hidden.reshape(-1, chan_count)
    grad_input = jnp.zeros((frame_total * row_count * col_count, chan_count), jnp.float32)
    tap_grads = []
    for tap_index in range(9):
        row_off, col_off = (tap_index // 3, tap_index % 3)
        window = padded_in[
            :, row_off : row_off + row_count, col_off : col_off + col_count, :
        ].reshape(-1, chan_count)
        tap_grads.append(
            lax.dot_general(window, grad_flat, CONTRACT_ROWS, preferred_element_type=jnp.float32)
        )
        flipped = padded_grad[
            :, 2 - row_off : 2 - row_off + row_count, 2 - col_off : 2 - col_off + col_count, :
        ].reshape(-1, chan_count)
        tap_weight = weights[tap_index * chan_count : (tap_index + 1) * chan_count]
        grad_input = grad_input + lax.dot_general(
            flipped, tap_weight, CONTRACT_COLS, preferred_element_type=jnp.float32
        )
    return (grad_input.reshape(frames.shape), jnp.concatenate(tap_grads, axis=0))


def norm_forward(hidden, norm_gain, norm_bias):
    frame_total, row_count, col_count, chan_count = hidden.shape
    grouped = hidden.astype(jnp.float32).reshape(
        frame_total, row_count * col_count, G, chan_count // G
    )
    group_mean = jnp.mean(grouped, axis=(1, 3), keepdims=True)
    centered = grouped - group_mean
    variance = jnp.mean(centered * centered, axis=(1, 3), keepdims=True)
    inv_std = lax.rsqrt(variance + EPSILON)
    normed = centered * inv_std
    preact = normed.reshape(hidden.shape) * norm_gain + norm_bias
    return (preact, normed, inv_std)


def norm_backward(grad_act, preact, normed, inv_std, norm_gain):
    sigmoid_z = jax.nn.sigmoid(preact)
    grad_pre = grad_act.astype(jnp.float32) * sigmoid_z * (1.0 + preact * (1.0 - sigmoid_z))
    grad_normed = (grad_pre * norm_gain).reshape(normed.shape)
    mean_grad = jnp.mean(grad_normed, axis=(1, 3), keepdims=True)
    mean_proj = jnp.mean(grad_normed * normed, axis=(1, 3), keepdims=True)
    return ((grad_normed - mean_grad - normed * mean_proj) * inv_std).reshape(preact.shape)


def temporal_backward(tiles, grad_out, w_time):
    clip_count, frame_total, pix_count, chan_count = tiles.shape
    grad_act = jnp.zeros(tiles.shape, jnp.float32)
    tap_grads = []
    for tap_index in range(3):
        kept = frame_total - tap_index
        earlier = tiles[:, :kept].reshape(-1, chan_count)
        later = grad_out[:, tap_index:].reshape(-1, chan_count)
        tap_grads.append(
            lax.dot_general(earlier, later, CONTRACT_ROWS, preferred_element_type=jnp.float32)
        )
        tap_weight = w_time[tap_index * chan_count : (tap_index + 1) * chan_count]
        back_part = lax.dot_general(
            later, tap_weight, CONTRACT_COLS, preferred_element_type=jnp.float32
        )
        back_part = back_part.reshape(clip_count, kept, pix_count, chan_count)
        grad_act = grad_act + jnp.pad(back_part, ((0, 0), (0, tap_index), (0, 0), (0, 0)))
    return (jnp.concatenate(tap_grads, axis=0), grad_act)


def shards(clips, w_spatial, w_time, norm_gain, norm_bias, grad_out):
    group_count, frame_count, row_count, col_count, chan_count = clips.shape
    frames = clips.reshape(group_count * frame_count, row_count, col_count, chan_count)
    weights = lax.all_gather(w_spatial, "dp", axis=1, tiled=True)
    hidden = spatial_forward(frames, weights).astype(jnp.bfloat16)
    preact, normed, inv_std = norm_forward(hidden, norm_gain, norm_bias)
    act = (
        jax.nn.silu(preact)
        .astype(jnp.bfloat16)
        .reshape(group_count, frame_count, row_count * col_count, chan_count)
    )
    tiles = lax.all_to_all(act, "wide", split_axis=2, concat_axis=1, tiled=True)
    tile_shape = tiles.shape
    by_clip = tiles.reshape(-1, FRAMES, tile_shape[2], tile_shape[3])
    grad_clipwise = grad_out.reshape(by_clip.shape)
    time_raw, grad_act = temporal_backward(by_clip, grad_clipwise, w_time)
    grad_act = grad_act.astype(jnp.bfloat16).reshape(tile_shape)
    returned = lax.all_to_all(grad_act, "wide", split_axis=1, concat_axis=2, tiled=True)
    grad_hidden = norm_backward(
        returned.reshape(frames.shape), preact, normed, inv_std, norm_gain
    ).astype(jnp.bfloat16)
    grad_input, spatial_raw = spatial_backward(frames, grad_hidden, weights)
    position_total = (
        group_count
        * frame_count
        * row_count
        * col_count
        * lax.axis_size("wide")
        * lax.axis_size("dp")
    )
    grad_scale = float(position_total) ** (-0.5)
    partial_pair = (
        lax.psum_scatter(spatial_raw, "wide", scatter_dimension=1, tiled=True),
        lax.psum_scatter(time_raw, "wide", scatter_dimension=1, tiled=True),
    )
    spatial_sum, time_sum = (
        lax.psum_scatter(partial_pair[0], "dp", scatter_dimension=0, tiled=True),
        lax.psum_scatter(partial_pair[1], "dp", scatter_dimension=0, tiled=True),
    )
    grad_clips = grad_input.astype(jnp.bfloat16).reshape(clips.shape)
    return (grad_clips, spatial_sum * grad_scale, time_sum * grad_scale)


def solution(mesh):
    return jax.shard_map(
        shards,
        mesh=mesh,
        in_specs=(
            P("dp", "wide", None, None, None),
            P(None, "dp"),
            P(),
            P(),
            P(),
            P("dp", None, "wide", None),
        ),
        out_specs=(P("dp", "wide", None, None, None), P("dp", "wide"), P("dp", "wide")),
        check_vma=False,
    )
```

profile of v0, /device:TPU:1, one launch (start us, length us, event | category | flops | bytes accessed | tf_op | source)
XLA Modules:
  0.0 496.7 jit_solution(4135765549354838031)
XLA Ops:
  7.9 1.3 copy.38
  9.2 2.1 pad_slice_fusion
  11.3 2.0 copy.39
  13.4 2.1 copy.40
  15.4 2.0 copy.41
  17.5 1.0 copy.42
  18.5 1.0 copy.43
  20.2 51.6 %all-gather.2.cloned.1.call-done = bf16[4608,512]{1,0:T(8,128)(2,1)} async-done(((bf16[4608,128]{1,0:T(8,128)(2,1)}), bf16[4608,512]{1,0:T(8,128)(2,1)}) %all-gather.2.cloned.1.call-update) | async-done | bytes 4718608 | tf_op jit(solution)/shard_map/all_gather | solution.py:104
  71.7 1.8 fusion.59
  73.5 1.7 convolution_add_fusion.15
  75.2 1.5 convolution_add_fusion.14
  76.8 1.5 convolution_add_fusion.13
  81.8 0.8 copy.63
  83.2 4.6 reduce.16
  87.8 2.0 reshape.573
  89.8 11.7 %all-to-all-start.1 = ((bf16[64,2,2048]{2,1,0:T(2,128)(2,1)}), bf16[64,2,2048]{2,1,0:T(2,128)(2,1)}, u32[]{:S(2)}, u32[]{:S(2)}) async-start(bf16[64,2,2048]{2,1,0:T(2,128)(2,1)} %reshape.573), calls=%async_computation.2 | async-start | bytes 1048576 | tf_op jit(solution)/shard_map/all_to_all | solution.py:112
  101.8 2.3 fusion.23
  104.2 2.4 fusion.25
  106.6 12.3 %all-to-all-done.1 = bf16[64,2,2048]{2,1,0:T(2,128)(2,1)} async-done(((bf16[64,2,2048]{2,1,0:T(2,128)(2,1)}), bf16[64,2,2048]{2,1,0:T(2,128)(2,1)}, u32[]{:S(2)}, u32[]{:S(2)}) %all-to-all-start.1) | async-done | bytes 524320 | tf_op jit(solution)/shard_map/all_to_all | solution.py:112
  118.8 3.6 reshape.574
  124.0 2.0 pad_maximum_fusion
  126.0 3.7 copy.58
  129.8 1.8 fusion.10
  131.5 23.4 %all_to_all.8 = bf16[1,64,8,512]{3,2,0,1:T(8,128)(2,1)S(1)} all-to-all(bf16[1,64,8,512]{3,2,0,1:T(8,128)(2,1)S(1)} %bitcast.223), channel_id=1, replica_groups=mesh['dp'=4,'wide'=64] {'wide'}, dimensions={1} | all-to-all | bytes 1048576 | tf_op jit(solution)/shard_map/all_to_all | solution.py:118
  157.0 1.5 fusion.8
  158.5 1.4 fusion.7
  159.9 1.5 fusion.6
  161.4 1.5 fusion.5
  162.9 2.0 fusion.4
  164.9 1.5 fusion.3
  166.4 1.5 fusion.2
  167.9 1.4 fusion.1
  169.3 1.5 fusion
  170.8 9.7 %copy.56 = f32[4608,512]{0,1:T(8,128)} copy(f32[4608,512]{1,0:T(8,128)} %fusion) | data formatting | bytes 18874368
  182.0 1.8 fusion.57
  183.8 1.5 convolution_add_fusion.7
  186.4 0.9 convolution_add_fusion.4
  188.2 74.9 %reduce-scatter.15.cloned.1.call-done = f32[8,1536]{1,0:T(8,128)} async-done(((f32[512,1536]{1,0:T(8,128)}), f32[8,1536]{1,0:T(8,128)}) %reduce-scatter.15.cloned.1.call-update) | async-done | bytes 49168
  263.1 2.0 copy.59
  265.2 1.5 convolution_add_fusion.1
  266.7 154.5 %reduce-scatter.13.cloned.1.call-done = f32[8,4608]{1,0:T(8,128)} async-done(((f32[512,4608]{1,0:T(8,128)}), f32[8,4608]{1,0:T(8,128)}) %reduce-scatter.13.cloned.1.call-update) | async-done | bytes 147472
  421.1 3.0 copy.57
  424.2 2.3 fusion.13
  426.5 24.1 %reduce-scatter.11.cloned.1.call-done = f32[384,8]{1,0:T(8,128)} async-done(((f32[1536,8]{1,0:T(8,128)}), f32[384,8]{1,0:T(8,128)}) %reduce-scatter.11.cloned.1.call-update) | async-done | bytes 12304 | tf_op jit(solution)/shard_map/reduce_scatter | solution.py:138
  450.5 0.9 broadcast_multiply_fusion.1
  452.2 36.1 %reduce-scatter.9.cloned.1.call-done = f32[1152,8]{1,0:T(8,128)} async-done(((f32[4608,8]{1,0:T(8,128)}), f32[1152,8]{1,0:T(8,128)}) %reduce-scatter.9.cloned.1.call-update) | async-done | bytes 36880 | tf_op jit(solution)/shard_map/reduce_scatter | solution.py:137
  488.2 1.1 broadcast_multiply_fusion
  489.3 0.8 copy.49
  (75 shorter events, 13.3 us)
Async XLA Ops:
  7.2 64.6 %all-gather.2.cloned.1.call-start = ((), (), s32[]{:S(2)}) async-start(), calls=%async_computation.6 | async-start | bytes 5898240 | tf_op jit(solution)/shard_map/all_gather | solution.py:104
  71.7 3.5 copy-start
  73.5 4.8 copy-start.3
  75.2 3.5 copy-start.5
  79.2 2.3 copy-start.6
  79.2 2.3 copy-start.7
  80.5 21.3 %copy-start.1 = (bf16[1,64,8,512]{3,2,1,0:T(8,128)(2,1)S(1)}, bf16[1,64,8,512]{3,2,1,0:T(8,128)(2,1)}, u32[]{:S(2)}) copy-start(bf16[1,64,8,512]{3,2,1,0:T(8,128)(2,1)} %param.11) | copy-start | bytes 1572868
  89.8 29.0 %all-to-all-start.1 = ((bf16[64,2,2048]{2,1,0:T(2,128)(2,1)}), bf16[64,2,2048]{2,1,0:T(2,128)(2,1)}, u32[]{:S(2)}, u32[]{:S(2)}) async-start(bf16[64,2,2048]{2,1,0:T(2,128)(2,1)} %reshape.573), calls=%async_computation.2 | async-start | bytes 1048576 | tf_op jit(solution)/shard_map/all_to_all | solution.py:112
  101.6 161.6 %reduce-scatter.15.cloned.1.call-start = ((), (), s32[]{:S(2)}) async-start(), calls=%async_computation.10 | async-start | bytes 3194880
  126.0 3.8 copy-start.2
  129.7 291.5 %reduce-scatter.13.cloned.1.call-start = ((), (), s32[]{:S(2)}) async-start(), calls=%async_computation.9 | async-start | bytes 9584640
  157.0 5.9 %copy-start.4 = (bf16[1,1,4,128,512]{4,3,2,1,0:T(8,128)(2,1)S(1)}, bf16[1,1,4,128,512]{4,3,2,1,0:T(8,128)(2,1)}, u32[]{:S(2)}) copy-start(bf16[1,1,4,128,512]{4,3,2,1,0:T(8,128)(2,1)} %param.6) | copy-start | bytes 1572868
  180.6 270.0 %reduce-scatter.11.cloned.1.call-start = ((), (), s32[]{:S(2)}) async-start(), calls=%async_computation.8 | async-start | bytes 983040 | tf_op jit(solution)/shard_map/reduce_scatter | solution.py:138
  180.8 4.5 slice-start
  181.5 3.8 slice-start.1
  265.1 223.1 %reduce-scatter.9.cloned.1.call-start = ((), (), s32[]{:S(2)}) async-start(), calls=%async_computation.7 | async-start | bytes 2949120 | tf_op jit(solution)/shard_map/reduce_scatter | solution.py:137
Sparse Core Ops, SparseCore 0:
  9.8 61.8 all-gather.1
  129.8 133.2 reduce-scatter.14
  267.4 153.6 reduce-scatter.12
  423.6 26.9 reduce-scatter.10
  452.9 35.2 reduce-scatter.8
where the time goes:
time: 498 us; the launch traced here: 497 us
  waiting for transfers between devices  354 us (71%)
  local copies, waits for them, and re-layouts  40.7 us (8%)
  matrix products  40.3 us (8%)
  blocking collectives  23.4 us (5%)
  between operations  14.2 us (3%)
  starting transfers between devices  12.4 us (2%)
  other arithmetic  11.7 us (2%)
    unnamed x7, waiting for transfers between devices  230 us
    all_gather x1, waiting for transfers between devices, shards(): weights = lax.all_gather(w_spatial, 'dp', axis=1, tiled=True)  51.6 us
    reduce_scatter x1, waiting for transfers between devices, shards(): lax.psum_scatter(partial_pair[0], 'dp', scatter_dimension=0, tiled=True)  36.1 us
    unnamed x31, local copies, waits for them, and re-layouts  27.6 us
    reduce_scatter x1, waiting for transfers between devices, shards(): lax.psum_scatter(partial_pair[1], 'dp', scatter_dimension=0, tiled=True)  24.1 us
    all_to_all x1, blocking collectives, shards(): lax.all_to_all(grad_act, 'wide', split_axis=1, concat_axis=2, tiled=True)  23.4 us
    dot_general x9, matrix products, spatial_backward(): lax.dot_general(window, grad_flat, CONTRACT_ROWS, preferred_element_type=...  13.8 us
    all_to_all x1, waiting for transfers between devices, shards(): tiles = lax.all_to_all(act, 'wide', split_axis=2, concat_axis=1, tiled=True)  12.3 us
  transfers between devices with their start and end apart: 6, of which 6 were waited for; matrix products, arithmetic and copies ran while one was open for 12% of the time, Pallas kernels for 0%

commit v1 on v0

v1 whole, which is shorter than its diff:
```python
import jax
import jax.numpy as jnp
from jax import lax
from jax.experimental import pallas as pl
from jax.experimental.pallas import tpu as pltpu
from jax.sharding import PartitionSpec as P

MESH = pl.DeviceIdType.MESH
F32 = jnp.float32
BF16 = jnp.bfloat16
EPSILON = 1e-06
CONTRACT_COLS = (((1,), (1,)), ((), ()))
NX, NY, NZ = 4, 4, 8
C = 512
PIX = 512
TAP_ROWS = 4608
HALF = TAP_ROWS // 2
PIECES = 3
PIECE = HALF // PIECES


def place():
    x = lax.axis_index("dp")
    w = lax.axis_index("wide")
    return x, w, w // 16, (w // 2) % 8, w % 2


def greet(partners):
    barrier = pltpu.get_barrier_semaphore()
    for partner in partners:
        pl.semaphore_signal(barrier, inc=1, device_id=partner, device_id_type=MESH)
    pl.semaphore_wait(barrier, len(partners))


def gather_kernel(
    w_ref, go_ref, w_out, go_out, slots,
    w_send, w_recv, f_send, f_recv, s_send, s_recv, y_send, y_recv, z_send, z_recv, e_send, e_recv, local_sem,
):
    x, w, y, z, c = place()
    way = 1 - 2 * c
    sibling = (x, w + way)
    ahead = (lax.rem(x + way + NX, NX), w)
    behind = (lax.rem(x - way + NX, NX), w)
    base = y * 16
    spot = lax.rem(w, 16)

    def ring_y(j):
        return (x, lax.rem(y + j, NY) * 16 + spot)

    def ring_z(k):
        return (x, base + lax.rem(spot + k, 16))

    greet([ahead, behind] + [ring_y(j) for j in range(1, NY)] + [ring_z(k) for k in range(1, 16)])

    def copy(src, dst, send, recv, target):
        return pltpu.make_async_remote_copy(
            src_ref=src, dst_ref=dst, send_sem=send, recv_sem=recv, device_id=target, device_id_type=MESH
        )

    def y_copy(j):
        frames = pl.ds(lax.rem(y + j, NY) * 16, 16)
        return copy(go_ref.at[frames], slots.at[j - 1], y_send.at[j - 1], y_recv.at[j - 1], ring_y(j))

    for j in range(1, NY):
        y_copy(j).start()

    def rows(core, piece):
        return pl.ds(pl.multiple_of(core * HALF + piece * PIECE, PIECE), PIECE)

    def cols(block):
        return pl.ds(pl.multiple_of(block * 128, 128), 128)

    def w_copy(side, piece):
        return copy(
            w_ref.at[rows(c, piece)], w_out.at[rows(c, piece), cols(x)],
            w_send.at[side, piece], w_recv.at[side, piece], ahead if side == 0 else behind,
        )

    for piece in range(PIECES):
        for side in range(2):
            w_copy(side, piece).start()

    own_w = pltpu.make_async_copy(w_ref, w_out.at[:, cols(x)], local_sem.at[NY])
    own_w.start()

    def z_source(j, start):
        if j == 0:
            return go_ref.at[pl.ds(base + start, 2)]
        return slots.at[j - 1, pl.ds(start, 2)]

    def from_y(j):
        return lax.rem(y - j + NY, NY)

    def z_copy(j, k):
        goal = lax.rem(spot + k, 16)
        core = lax.rem(goal, 2)
        start = goal // 2 * 2 + 2 * core
        return copy(
            z_source(j, start), go_out.at[pl.ds(core, 2), from_y(j), spot],
            z_send.at[j, k - 1], z_recv.at[j, k - 1], ring_z(k),
        )

    def wanted(goal):
        return jnp.logical_or(lax.rem(goal, 2) == 0, lax.rem(goal // 2, 4) != 3)

    keeps = wanted(spot)

    def own_go(j):
        start = z * 2 + 2 * c
        return pltpu.make_async_copy(
            z_source(j, start), go_out.at[pl.ds(c, 2), from_y(j), spot], local_sem.at[j]
        )

    for j in range(NY):
        if j > 0:
            y_copy(j).wait_recv()

        @pl.when(keeps)
        def _():
            own_go(j).start()

        def begin(k, carry):
            @pl.when(wanted(lax.rem(spot + k, 16)))
            def _():
                z_copy(j, k).start()

            return carry

        lax.fori_loop(1, 16, begin, 0)

    def f_copy(piece):
        place_of = w_out.at[rows(c, piece), cols(behind[0])]
        return copy(place_of, place_of, f_send.at[piece], f_recv.at[piece], ahead)

    def s_copy(index, piece):
        block = (behind[0], ahead[0], lax.rem(x + 2, NX))[index]
        place_of = w_out.at[rows(c, piece), cols(block)]
        return copy(place_of, place_of, s_send.at[index, piece], s_recv.at[index, piece], sibling)

    for piece in range(PIECES):
        w_copy(0, piece).wait_recv()
        f_copy(piece).start()
        s_copy(0, piece).start()
        w_copy(1, piece).wait_recv()
        s_copy(1, piece).start()
    for piece in range(PIECES):
        f_copy(piece).wait_recv()
        s_copy(2, piece).start()

    @pl.when(keeps)
    def _():
        for j in range(NY):
            own_go(j).wait()

            def arrive(k, carry):
                source = lax.rem(spot - k + 16, 16)
                landed = go_out.at[pl.ds(c, 2), from_y(j), source]
                copy(landed, landed, z_send.at[j, k - 1], z_recv.at[j, k - 1], ring_z(k)).wait_recv()
                return carry

            lax.fori_loop(1, 16, arrive, 0)

    def e_copy():
        return copy(go_out.at[1], go_out.at[2 * c], e_send, e_recv, sibling)

    whole = lax.rem(z, 4) != 3

    @pl.when(keeps)
    def _():
        e_copy().start()

    @pl.when(jnp.logical_or(c == 1, whole))
    def _():
        e_copy().wait_recv()

    for index in range(3):
        for piece in range(PIECES):
            s_copy(index, piece).wait_recv()

    own_w.wait()
    for j in range(1, NY):
        y_copy(j).wait_send()
    for piece in range(PIECES):
        w_copy(0, piece).wait_send()
        w_copy(1, piece).wait_send()
        f_copy(piece).wait_send()
        for index in range(3):
            s_copy(index, piece).wait_send()

    @pl.when(keeps)
    def _():
        e_copy().wait_send()

    for j in range(NY):

        def leave(k, carry):
            @pl.when(wanted(lax.rem(spot + k, 16)))
            def _():
                z_copy(j, k).wait_send()

            return carry

        lax.fori_loop(1, 16, leave, 0)


def gather_inputs(w_spatial, grad_out):
    anywhere = pl.BlockSpec(memory_space=pl.ANY)
    dma = pltpu.SemaphoreType.DMA
    return pl.pallas_call(
        gather_kernel,
        out_shape=(
            jax.ShapeDtypeStruct((TAP_ROWS, C), BF16),
            jax.ShapeDtypeStruct((3, NY, 16, 8, C), BF16),
            jax.ShapeDtypeStruct((NY - 1, 16, 8, C), BF16),
        ),
        in_specs=[anywhere] * 2,
        out_specs=(anywhere,) * 3,
        scratch_shapes=[
            dma((2, PIECES)), dma((2, PIECES)), dma((PIECES,)), dma((PIECES,)), dma((3, PIECES)), dma((3, PIECES)),
            dma((NY - 1,)), dma((NY - 1,)), dma((NY, 15)), dma((NY, 15)), dma, dma, dma((NY + 1,)),
        ],
        compiler_params=pltpu.CompilerParams(collective_id=0, has_side_effects=True),
        name="gather_inputs",
    )(w_spatial, grad_out)


def group_sum(values):
    lane = lax.broadcasted_iota(jnp.int32, values.shape, 1)
    total = values.shape[1]
    for step in (1, 2, 4, 8):
        upper = lax.rem(lane // step, 2) == 1
        values = values + jnp.where(upper, pltpu.roll(values, step, 1), pltpu.roll(values, total - step, 1))
    return values


def group_mean(full):
    by_chan = jnp.sum(full, axis=0, keepdims=True)
    return group_sum(jnp.broadcast_to(by_chan, (8, C)))[0:1] * (1.0 / (16 * PIX))


def shifted(values):
    col = lax.rem(lax.broadcasted_iota(jnp.int32, (PIX, C), 0), 128)
    before = jnp.where(col == 0, 0.0, pltpu.roll(values, 1, 0))
    after = jnp.where(col == 127, 0.0, pltpu.roll(values, PIX - 1, 0))
    return before.astype(BF16), after.astype(BF16)


def block_kernel(
    x_ref, w_ref, wt_ref, gain_ref, bias_ref, go_ref, gx_ref, p_ref, q_ref, r_ref, xs, gs, acc, time_part
):
    pos = lax.rem(lax.axis_index("wide"), 8)
    edge = jnp.zeros((128, 3 * C), BF16)
    xs[0:128, :] = edge
    xs[640:768, :] = edge
    gs[0:128, :] = edge
    gs[640:768, :] = edge
    before, after = shifted(x_ref[...].astype(F32))
    xs[128:640, 0:C] = before
    xs[128:640, C : 2 * C] = x_ref[...]
    xs[128:640, 2 * C :] = after
    hidden = jnp.zeros((PIX, C), F32)
    for a in range(3):
        hidden = hidden + jnp.dot(
            xs[128 * a : 128 * a + PIX, :], w_ref[1536 * a : 1536 * a + 1536, :], preferred_element_type=F32
        )
    hidden = hidden.astype(BF16).astype(F32)
    gain = gain_ref[...]
    centered = hidden - group_mean(hidden)
    inv_std = lax.rsqrt(group_mean(centered * centered) + EPSILON)
    normed = centered * inv_std
    preact = normed * gain + bias_ref[...]
    sig = jax.nn.sigmoid(preact)
    act = (preact * sig).astype(BF16)

    grad_act = jnp.zeros((PIX, C), F32)
    for k in range(3):
        later = go_ref[k].astype(F32)
        if k > 0:
            later = jnp.where(pos + k < 8, later, 0.0)
        later = later.astype(BF16)
        grad_act = grad_act + lax.dot_general(
            later, wt_ref[C * k : C * k + C, :], CONTRACT_COLS, preferred_element_type=F32
        )
        time_part[:, C * k : C * k + C] = jnp.dot(later.T, act, preferred_element_type=F32)
    grad_act = grad_act.astype(BF16).astype(F32)
    grad_normed = grad_act * sig * (1.0 + preact * (1.0 - sig)) * gain
    grad_hidden = (grad_normed - group_mean(grad_normed) - normed * group_mean(grad_normed * normed)) * inv_std
    grad_low = grad_hidden.astype(BF16)
    before, after = shifted(grad_low.astype(F32))
    gs[128:640, 0:C] = after
    gs[128:640, C : 2 * C] = grad_low
    gs[128:640, 2 * C :] = before
    for a in range(3):
        for b in range(3):
            tap = 3 * a + b
            part = lax.dot_general(
                gs[128 * (2 - a) : 128 * (2 - a) + PIX, C * b : C * b + C],
                w_ref[C * tap : C * tap + C, :],
                CONTRACT_COLS,
                preferred_element_type=F32,
            )
            if tap == 0:
                acc[...] = part
            elif tap < 8:
                acc[...] += part
            else:
                gx_ref[...] = (acc[...] + part).astype(BF16)

    flipped = grad_low.T
    for i in range(NX):
        chunks = []
        for n in range(3 * i, 3 * i + 3):
            a, col = n // 4, 384 * (n % 4)
            chunk = jnp.dot(flipped, xs[128 * a : 128 * a + PIX, col : col + 384], preferred_element_type=F32)
            chunks.append(chunk.reshape(32, 2, 8, 384))
        chunks.append(time_part[:, 384 * i : 384 * i + 384].reshape(32, 2, 8, 384))
        for core in range(2):
            s0, s1, s2, t0 = [chunk[:, core] for chunk in chunks]
            p_ref[core, i] = jnp.concatenate([s0, s1], axis=1).astype(BF16).reshape(NY, NZ, 16, 384)
            rest = jnp.concatenate([s2, t0], axis=1).astype(BF16).reshape(NY, NZ, 16, 384)
            for y in range(NY):
                q_ref[core, y, i] = rest[y, :, :, :256]
                for z in range(NZ):
                    r_ref[core, z, y, i] = rest[y, z, :, 256:]


def block_pass(frames, weights, w_time, gain, bias, later):
    vmem = pl.BlockSpec(memory_space=pltpu.VMEM)
    return pl.pallas_call(
        block_kernel,
        out_shape=(
            jax.ShapeDtypeStruct((PIX, C), BF16),
            jax.ShapeDtypeStruct((2, NX, NY, NZ, 16, 384), BF16),
            jax.ShapeDtypeStruct((2, NY, NX, NZ, 16, 256), BF16),
            jax.ShapeDtypeStruct((2, NZ, NY, NX, 16, 128), BF16),
        ),
        in_specs=[vmem] * 6,
        out_specs=(vmem,) * 4,
        scratch_shapes=[
            pltpu.VMEM((768, 3 * C), BF16),
            pltpu.VMEM((768, 3 * C), BF16),
            pltpu.VMEM((PIX, C), F32),
            pltpu.VMEM((C, 3 * C), F32),
        ],
        compiler_params=pltpu.CompilerParams(vmem_limit_bytes=48 * 1024 * 1024),
        name="block_pass",
    )(frames, weights, w_time, gain, bias, later)


ORDERS = (("x", "y", "z"), ("y", "x", "z"), ("z", "y", "x"))
SIZES = {"x": NX, "y": NY, "z": NZ}
LANES = (384, 256, 128)


def sum_kernel(scale, *refs):
    ins, (spatial_ref, time_ref), refs = refs[:3], refs[3:5], refs[5:]
    x, w, y, z, c = place()
    at = {"x": x, "y": y, "z": z}

    def partner(axis, k):
        moved = dict(at)
        moved[axis] = lax.rem(at[axis] + k, SIZES[axis])
        return (moved["x"], moved["y"] * 16 + moved["z"] * 2 + c)

    sibling = (x, w + 1 - 2 * c)
    greet([sibling] + [partner(axis, k) for axis in "xyz" for k in range(1, SIZES[axis])])

    def copy(src, dst, send, recv, target):
        return pltpu.make_async_remote_copy(
            src_ref=src, dst_ref=dst, send_sem=send, recv_sem=recv, device_id=target, device_id_type=MESH
        )

    class Part:
        pass

    parts = []
    for index in range(3):
        part = Part()
        part.source = ins[index]
        part.order = ORDERS[index]
        (part.pair, part.go1, part.got1, part.sum1, part.go2, part.got2, part.sum2, part.go3, part.got3,
         part.pair_sems, part.sems1, part.sems2, part.sems3) = refs[13 * index : 13 * index + 13]
        part.pair_copy = copy(
            part.source.at[1 - c], part.pair, part.pair_sems.at[0], part.pair_sems.at[1], sibling
        )
        parts.append(part)

    def hop(part, level, k):
        axis = part.order[level]
        sends = (part.go1, part.go2, part.go3)[level]
        lands = (part.got1, part.got2, part.got3)[level]
        sems = (part.sems1, part.sems2, part.sems3)[level]
        goal = lax.rem(at[axis] + k, SIZES[axis])
        return copy(sends.at[goal], lands.at[k - 1], sems.at[0, k - 1], sems.at[1, k - 1], partner(axis, k))

    sequence = (2, 0, 1)
    for index in sequence:
        parts[index].pair_copy.start()
    for index in sequence:
        part = parts[index]
        part.pair_copy.wait_recv()
        axis = part.order[0]
        for k in range(1, SIZES[axis]):
            goal = lax.rem(at[axis] + k, SIZES[axis])
            part.go1[goal] = (part.source[c, goal].astype(F32) + part.pair[goal].astype(F32)).astype(BF16)
            hop(part, 0, k).start()
    for index in (1, 2, 0):
        part = parts[index]
        mine = at[part.order[0]]
        total = part.source[c, mine].astype(F32) + part.pair[mine].astype(F32)
        for k in range(1, SIZES[part.order[0]]):
            hop(part, 0, k).wait_recv()
            total = total + part.got1[k - 1].astype(F32)
        part.sum1[...] = total
        part.go2[...] = total.astype(BF16)
        for k in range(1, SIZES[part.order[1]]):
            hop(part, 1, k).start()
    for index in (1, 2, 0):
        part = parts[index]
        total = part.sum1[at[part.order[1]]]
        for k in range(1, SIZES[part.order[1]]):
            hop(part, 1, k).wait_recv()
            total = total + part.got2[k - 1].astype(F32)
        part.sum2[...] = total
        part.go3[...] = total.astype(BF16)
        for k in range(1, SIZES[part.order[2]]):
            hop(part, 2, k).start()
    results = [None] * 3
    for index in (1, 2, 0):
        part = parts[index]
        total = part.sum2[at[part.order[2]]]
        for k in range(1, SIZES[part.order[2]]):
            hop(part, 2, k).wait_recv()
            total = total + part.got3[k - 1].astype(F32)
        results[index] = total * scale
    first, second, third = results
    spatial_ref[:, 0:384] = first[0:8]
    spatial_ref[:, 384:768] = first[8:16]
    spatial_ref[:, 768:1024] = second[0:8]
    spatial_ref[:, 1024:1152] = third[0:8]
    time_ref[:, 0:256] = second[8:16]
    time_ref[:, 256:384] = third[8:16]
    for part in parts:
        part.pair_copy.wait_send()
        for level in range(3):
            for k in range(1, SIZES[part.order[level]]):
                hop(part, level, k).wait_send()


def sum_partials(parts, scale):
    vmem = pl.BlockSpec(memory_space=pltpu.VMEM)
    dma = pltpu.SemaphoreType.DMA
    scratch = []
    for order, lanes in zip(ORDERS, LANES):
        n1, n2, n3 = [SIZES[axis] for axis in order]
        scratch += [
            pltpu.VMEM((n1, n2, n3, 16, lanes), BF16),
            pltpu.VMEM((n1, n2, n3, 16, lanes), BF16),
            pltpu.VMEM((n1 - 1, n2, n3, 16, lanes), BF16),
            pltpu.VMEM((n2, n3, 16, lanes), F32),
            pltpu.VMEM((n2, n3, 16, lanes), BF16),
            pltpu.VMEM((n2 - 1, n3, 16, lanes), BF16),
            pltpu.VMEM((n3, 16, lanes), F32),
            pltpu.VMEM((n3, 16, lanes), BF16),
            pltpu.VMEM((n3 - 1, 16, lanes), BF16),
            dma((2,)),
            dma((2, n1 - 1)),
            dma((2, n2 - 1)),
            dma((2, n3 - 1)),
        ]

    def kernel(*refs):
        sum_kernel(scale, *refs)

    return pl.pallas_call(
        kernel,
        out_shape=(jax.ShapeDtypeStruct((8, 1152), F32), jax.ShapeDtypeStruct((8, 384), F32)),
        in_specs=[vmem] * 3,
        out_specs=(vmem,) * 2,
        scratch_shapes=scratch,
        compiler_params=pltpu.CompilerParams(
            collective_id=1, has_side_effects=True, vmem_limit_bytes=48 * 1024 * 1024
        ),
        name="sum_partials",
    )(*parts)


def shards(clips, w_spatial, w_time, norm_gain, norm_bias, grad_out):
    weights, later, _ = gather_inputs(w_spatial, grad_out.reshape(64, 8, C))
    grad_clips, *partials = block_pass(
        clips.reshape(PIX, C),
        weights,
        w_time,
        norm_gain.reshape(1, C),
        norm_bias.reshape(1, C),
        later.reshape(3, PIX, C),
    )
    scale = float(PIX * 64 * NX) ** (-0.5)
    spatial, time = sum_partials(partials, scale)
    return grad_clips.reshape(clips.shape), spatial.T, time.T


def solution(mesh):
    return jax.shard_map(
        shards,
        mesh=mesh,
        in_specs=(
            P("dp", "wide", None, None, None),
            P(None, "dp"),
            P(),
            P(),
            P(),
            P("dp", None, "wide", None),
        ),
        out_specs=(P("dp", "wide", None, None, None), P("dp", "wide"), P("dp", "wide")),
        check_vma=False,
    )
```

time: 498 us -> 119 us (0.24)
  waiting for transfers between devices: 354 us -> 0 us
  Pallas kernels: 0 us -> 111 us
  matrix products: 40.3 us -> 0 us
  local copies, waits for them, and re-layouts: 40.7 us -> 6.62 us
  blocking collectives: 23.4 us -> 0 us
  between operations: 14.2 us -> 0.68 us
  starting transfers between devices: 12.4 us -> 0 us
  other arithmetic: 11.7 us -> 0 us
    unnamed x7 -> x0, waiting for transfers between devices: 230 us -> none
    pallas_call x0 -> x3, Pallas kernels: none -> 111 us  [the longest x1 52.5 us: gather_inputs(): pl.pallas_call(gather_kernel, out_shape=(jax.ShapeDtypeStruct((TAP_ROWS,...]
    reduce_scatter x2 -> x0, waiting for transfers between devices: 60.1 us -> none  [the longest x1 36.1 us: shards(): lax.psum_scatter(partial_pair[0], 'dp', scatter_dimension=0, tiled=True)]
    all_gather x1 -> x0, waiting for transfers between devices: 51.6 us -> none  [shards(): weights = lax.all_gather(w_spatial, 'dp', axis=1, tiled=True)]
    dot_general x33 -> x0, matrix products: 40.3 us -> none  [the longest x9 13.8 us: spatial_backward(): lax.dot_general(window, grad_flat, CONTRACT_ROWS, preferred_element_type=...]
    all_to_all x1 -> x0, blocking collectives: 23.4 us -> none  [shards(): lax.all_to_all(grad_act, 'wide', split_axis=1, concat_axis=2, tiled=True)]
    unnamed x31 -> x14, local copies, waits for them, and re-layouts: 27.6 us -> 6.62 us
    all_to_all x1 -> x0, waiting for transfers between devices: 12.3 us -> none  [shards(): tiles = lax.all_to_all(act, 'wide', split_axis=2, concat_axis=1, tiled=True)]
  transfers between devices with their start and end apart: 6 -> 0, of which waited for: 6 -> 0; matrix products, arithmetic and copies ran while one was open for 12% -> 0% of each run, Pallas kernels for 0% -> 0%
where the time goes in v1:
time: 119 us; the launch traced here: 118 us
  Pallas kernels  111 us (93%)
  local copies, waits for them, and re-layouts  6.62 us (6%)
    pallas_call x1, Pallas kernels, gather_inputs(): pl.pallas_call(gather_kernel, out_shape=(jax.ShapeDtypeStruct((TAP_ROWS,...  52.5 us
    pallas_call x1, Pallas kernels, sum_partials(): pl.pallas_call(kernel, out_shape=(jax.ShapeDtypeStruct((8, 1152), F32), j...  42.4 us
    pallas_call x1, Pallas kernels, block_pass(): pl.pallas_call(block_kernel, out_shape=(jax.ShapeDtypeStruct((PIX, C), BF...  16.1 us
    unnamed x14, local copies, waits for them, and re-layouts  6.62 us

profile of v1, /device:TPU:1, one launch (start us, length us, event | category | flops | bytes accessed | tf_op | source)
XLA Modules:
  0.0 118.3 jit_solution(17327232987226158315)
XLA Ops:
  0.6 0.0 copy-start.1
  0.6 52.5 %gather_inputs.1 = (bf16[4608,512]{1,0:T(8,128)(2,1)}, bf16[3,4,16,8,512]{4,3,2,1,0:T(8,128)(2,1)}, bf16[3,16,8,512]{3,2,1,0:T(8,128)(2,1)}) custom-call(bf16[4608,128]{1,0:T(8,128)(2,1)} %w_ref.1, bf16[64,8,512]{2,1,0:T(8,128)(2,1)} %bitcast.14), custom_call_target="tpu_custom_call" | custom-call | tf_op jit(solution)/shard_map/gather_inputs/pallas_call | solution.py:209
  53.1 0.0 copy-done.1
  53.1 0.0 copy-start.2
  53.2 1.4 %copy-done.2 = bf16[3,4,16,8,512]{4,3,2,1,0:T(8,128)(2,1)S(1)} copy-done((bf16[3,4,16,8,512]{4,3,2,1,0:T(8,128)(2,1)S(1)}, bf16[3,4,16,8,512]{4,3,2,1,0:T(8,128)(2,1)}, u32[]{:S(2)}) %copy-start.2) | copy-done | bytes 1572888
  54.6 0.0 copy-start.3
  54.6 1.0 copy-done.3
  55.6 0.0 copy-start.4
  55.6 0.7 copy-done.4
  56.3 0.0 copy-start.5
  56.3 0.7 copy-done.5
  57.0 16.1 %block_pass.1 = (bf16[512,512]{1,0:T(8,128)(2,1)}, bf16[2,4,4,8,16,384]{5,4,3,2,1,0:T(8,128)(2,1)}, bf16[2,4,4,8,16,256]{5,4,3,2,1,0:T(8,128)(2,1)}, bf16[2,8,4,4,16,128]{5,4,3,2,1,0:T(8,128)(2,1)S(1)}) custom-call(bf16[512,512]{1,0:T(8,128)(2,1)S(1)} %bitcast.9, bf16[4608,512]{1,0:T(8,128)(2,1)} %get-tuple-element.11.w_ref, ...), custom_call_target="tpu_custom_call" | custom-call | tf_op jit(solution)/shard_map/block_pass/pallas_call | solution.py:329
  73.1 0.0 copy-start
  73.1 1.6 %copy-done = bf16[2,4,4,8,16,256]{5,4,3,2,1,0:T(8,128)(2,1)S(1)} copy-done((bf16[2,4,4,8,16,256]{5,4,3,2,1,0:T(8,128)(2,1)S(1)}, bf16[2,4,4,8,16,256]{5,4,3,2,1,0:T(8,128)(2,1)}, u32[]{:S(2)}) %copy-start) | copy-done | bytes 2097176
  74.7 42.4 %sum_partials.1 = (f32[8,1152]{1,0:T(8,128)S(1)}, f32[8,384]{1,0:T(8,128)S(1)}) custom-call(bf16[2,4,4,8,16,384]{5,4,3,2,1,0:T(8,128)(2,1)} %get-tuple-element.14.refs_0_, bf16[2,4,4,8,16,256]{5,4,3,2,1,0:T(8,128)(2,1)S(1)} %copy-done, bf16[2,8,4,4,16,128]{5,4,3,2,1,0:T(8,128)(2,1)S(1)} %get-tuple-element.16.refs_2_), custom_call_target="tpu_custom_call" | custom-call | tf_op jit(solution)/shard_map/sum_partials/pallas_call | solution.py:475
  117.1 0.6 copy.11
  117.7 0.6 copy.12
Async XLA Ops:
  0.6 52.5 %copy-start.1 = (bf16[1536,512]{1,0:T(8,128)(2,1)S(1)}, bf16[1536,512]{1,0:T(8,128)(2,1)}, u32[]{:S(2)}) copy-start(bf16[1536,512]{1,0:T(8,128)(2,1)} %wt_ref.1) | copy-start | bytes 4718596
  53.1 1.4 %copy-start.2 = (bf16[3,4,16,8,512]{4,3,2,1,0:T(8,128)(2,1)S(1)}, bf16[3,4,16,8,512]{4,3,2,1,0:T(8,128)(2,1)}, u32[]{:S(2)}) copy-start(bf16[3,4,16,8,512]{4,3,2,1,0:T(8,128)(2,1)} %get-tuple-element.12) | copy-start | bytes 4718596
  54.6 1.0 copy-start.3
  55.6 0.7 copy-start.4
  56.3 0.7 copy-start.5
  73.1 1.6 %copy-start = (bf16[2,4,4,8,16,256]{5,4,3,2,1,0:T(8,128)(2,1)S(1)}, bf16[2,4,4,8,16,256]{5,4,3,2,1,0:T(8,128)(2,1)}, u32[]{:S(2)}) copy-start(bf16[2,4,4,8,16,256]{5,4,3,2,1,0:T(8,128)(2,1)} %get-tuple-element.15.refs_1_) | copy-start | bytes 6291460

commit v2 on v0

v2 whole, which is shorter than its diff:
```python
import jax
import jax.numpy as jnp
from jax import lax
from jax.experimental import pallas as pl
from jax.experimental.pallas import tpu as pltpu
from jax.sharding import PartitionSpec as P

MESH = pl.DeviceIdType.MESH
F32 = jnp.float32
BF16 = jnp.bfloat16
EPSILON = 1e-06
CONTRACT_COLS = (((1,), (1,)), ((), ()))
NX, NY, NZ = 4, 4, 8
C = 512
PIX = 512
TAP_ROWS = 4608
PIECES = 3
PIECE = TAP_ROWS // PIECES // 2
SIZES = {"x": NX, "y": NY, "z": NZ}
ORDERS = (("x", "y", "z"), ("y", "x", "z"), ("z", "y", "x"))
LANES = (384, 256, 128)


def place():
    x = lax.axis_index("dp")
    w = lax.axis_index("wide")
    return x, w, w // 16, (w // 2) % 8, w % 2


def greet(partners):
    barrier = pltpu.get_barrier_semaphore()
    for partner in partners:
        pl.semaphore_signal(barrier, inc=1, device_id=partner, device_id_type=MESH)
    pl.semaphore_wait(barrier, len(partners))


def group_sum(values):
    lane = lax.broadcasted_iota(jnp.int32, values.shape, 1)
    total = values.shape[1]
    for step in (1, 2, 4, 8):
        upper = lax.rem(lane // step, 2) == 1
        values = values + jnp.where(upper, pltpu.roll(values, step, 1), pltpu.roll(values, total - step, 1))
    return values


def group_mean(full):
    by_chan = jnp.sum(full, axis=0, keepdims=True)
    return group_sum(jnp.broadcast_to(by_chan, (8, C)))[0:1] * (1.0 / (16 * PIX))


def shifted(values):
    col = lax.rem(lax.broadcasted_iota(jnp.int32, (PIX, C), 0), 128)
    before = jnp.where(col == 0, 0.0, pltpu.roll(values, 1, 0))
    after = jnp.where(col == 127, 0.0, pltpu.roll(values, PIX - 1, 0))
    return before.astype(BF16), after.astype(BF16)


def copy(src, dst, send, recv, target):
    return pltpu.make_async_remote_copy(
        src_ref=src, dst_ref=dst, send_sem=send, recv_sem=recv, device_id=target, device_id_type=MESH
    )


def own_rows(values, core):
    split = values.reshape(32, 2, 8, values.shape[1])
    return jnp.where(core == 0, split[:, 0], split[:, 1]).reshape(256, values.shape[1]).astype(BF16)


class Part:
    pass


def block_kernel(scale, *refs):
    (x_ref, w_ref, wt_ref, gain_ref, bias_ref, go_ref, gx_ref, spatial_ref, time_ref) = refs[:9]
    (weights, w_time, frames, windows, grad_windows, landed, slots, later, later_rows, acts, grads, grad_rows, acc,
     time_part, gx_low) = refs[9:24]
    (w_send, w_recv, f_send, f_recv, s_send, s_recv, y_send, y_recv, z_send, z_recv, e_sems, pair_sems,
     local_sem) = refs[24:37]
    part_refs = refs[37:]

    x, w, y, z, c = place()
    at = {"x": x, "y": y, "z": z}
    way = 1 - 2 * c
    sibling = (x, w + way)
    ahead = (lax.rem(x + way + NX, NX), w)
    behind = (lax.rem(x - way + NX, NX), w)
    base = y * 16
    spot = lax.rem(w, 16)

    def partner(axis, k):
        moved = dict(at)
        moved[axis] = lax.rem(at[axis] + k, SIZES[axis])
        return (moved["x"], moved["y"] * 16 + moved["z"] * 2 + c)

    def ring_y(j):
        return partner("y", j)

    def ring_z(k):
        return (x, base + lax.rem(spot + k, 16))

    loads = [
        pltpu.make_async_copy(x_ref, frames.at[c], local_sem.at[5]),
        pltpu.make_async_copy(wt_ref, w_time, local_sem.at[6]),
    ]
    for load in loads:
        load.start()
    greet(
        [partner("x", k) for k in range(1, NX)]
        + [ring_y(j) for j in range(1, NY)]
        + [ring_z(k) for k in range(1, 16)]
    )

    def rows(core, piece):
        return pl.ds(pl.multiple_of((2 * piece + core) * PIECE, PIECE), PIECE)

    def cols(block):
        return pl.ds(pl.multiple_of(block * 128, 128), 128)

    def w_copy(side, piece):
        return copy(
            w_ref.at[rows(c, piece)], weights.at[rows(c, piece), cols(x)],
            w_send.at[side, piece], w_recv.at[side, piece], ahead if side == 0 else behind,
        )

    def f_copy(piece):
        spot_of = weights.at[rows(c, piece), cols(behind[0])]
        return copy(spot_of, spot_of, f_send.at[piece], f_recv.at[piece], ahead)

    def s_copy(index, piece):
        block = (behind[0], ahead[0], lax.rem(x + 2, NX))[index]
        spot_of = weights.at[rows(c, piece), cols(block)]
        return copy(spot_of, spot_of, s_send.at[index, piece], s_recv.at[index, piece], sibling)

    def y_copy(j):
        source = pl.ds(lax.rem(y + j, NY) * 16, 16)
        return copy(go_ref.at[source], slots.at[j - 1], y_send.at[j - 1], y_recv.at[j - 1], ring_y(j))

    def z_source(j, start):
        if j == 0:
            return go_ref.at[pl.ds(base + start, 2)]
        return slots.at[j - 1, pl.ds(start, 2)]

    def from_y(j):
        return lax.rem(y - j + NY, NY)

    def z_copy(j, k):
        goal = lax.rem(spot + k, 16)
        core = lax.rem(goal, 2)
        start = goal // 2 * 2 + 2 * core
        return copy(
            z_source(j, start), landed.at[pl.ds(2 * core, 2), from_y(j), spot],
            z_send.at[j, k - 1], z_recv.at[j, k - 1], ring_z(k),
        )

    def wanted(goal):
        return jnp.logical_or(lax.rem(goal, 2) == 0, lax.rem(goal // 2, 4) != 3)

    keeps = wanted(spot)
    whole = lax.rem(z, 4) != 3

    def own_go(j):
        start = z * 2 + 2 * c
        return pltpu.make_async_copy(
            z_source(j, start), landed.at[pl.ds(2 * c, 2), from_y(j), spot], local_sem.at[j]
        )

    def z_start(j):
        if j > 0:
            y_copy(j).wait_recv()

        @pl.when(keeps)
        def _():
            own_go(j).start()

        def begin(k, carry):
            @pl.when(wanted(lax.rem(spot + k, 16)))
            def _():
                z_copy(j, k).start()

            return carry

        lax.fori_loop(1, 16, begin, 0)

    def pair_copy(index, array):
        return copy(array.at[c], array.at[c], pair_sems.at[0, index], pair_sems.at[1, index], sibling)

    for piece in range(PIECES):
        for side in range(2):
            w_copy(side, piece).start()
    for j in (2, 1, 3):
        y_copy(j).start()
    z_start(0)
    own_w = pltpu.make_async_copy(w_ref, weights.at[:, cols(x)], local_sem.at[4])
    own_w.start()
    loads[0].wait()
    pair_copy(0, frames).start()
    edge = jnp.zeros((128, 3 * C), BF16)

    def fill(target, values, low, flip):
        before, after = shifted(values)
        target[0:128, :] = edge
        target[640:768, :] = edge
        target[128:640, 0:C] = after if flip else before
        target[128:640, C : 2 * C] = low
        target[128:640, 2 * C :] = before if flip else after

    fill(windows.at[c], frames[c].astype(F32), frames[c], False)
    w_copy(0, 0).wait_recv()
    f_copy(0).start()
    s_copy(0, 0).start()
    w_copy(1, 0).wait_recv()
    s_copy(1, 0).start()
    z_start(1)
    z_start(3)
    for piece in range(1, PIECES):
        w_copy(0, piece).wait_recv()
        f_copy(piece).start()
        s_copy(0, piece).start()
        w_copy(1, piece).wait_recv()
        s_copy(1, piece).start()
        if piece == 1:
            z_start(2)
    own_w.wait()

    def forward(a):
        for index in range(3):
            s_copy(index, a).wait_recv()
        part = jnp.dot(
            windows[c, 128 * a : 128 * a + PIX, :], weights[1536 * a : 1536 * a + 1536, :], preferred_element_type=F32
        )
        if a == 0:
            acc[...] = part
        else:
            acc[...] += part

    for piece in range(PIECES):
        f_copy(piece).wait_recv()
        s_copy(2, piece).start()
        if piece > 0:
            forward(piece - 1)
    forward(PIECES - 1)
    hidden = acc[...].astype(BF16).astype(F32)
    gain = gain_ref[...]
    centered = hidden - group_mean(hidden)
    inv_std = lax.rsqrt(group_mean(centered * centered) + EPSILON)
    normed = centered * inv_std
    preact = normed * gain + bias_ref[...]
    sig = jax.nn.sigmoid(preact)
    acts[c] = (preact * sig).astype(BF16)
    pair_copy(1, acts).start()
    slope = sig * (1.0 + preact * (1.0 - sig)) * gain

    pair_copy(0, frames).wait_recv()
    fill(windows.at[1 - c], frames[1 - c].astype(F32), frames[1 - c], False)

    @pl.when(keeps)
    def _():
        for j in range(NY):
            own_go(j).wait()

            def arrive(k, carry):
                source = lax.rem(spot - k + 16, 16)
                place_of = landed.at[pl.ds(2 * c, 2), from_y(j), source]
                copy(place_of, place_of, z_send.at[j, k - 1], z_recv.at[j, k - 1], ring_z(k)).wait_recv()
                return carry

            lax.fori_loop(1, 16, arrive, 0)

    def e_copy():
        both = landed.at[pl.ds(2 * c, 2)]
        return copy(both, both, e_sems.at[0], e_sems.at[1], sibling)

    @pl.when(keeps)
    def _():
        e_copy().start()

    @pl.when(jnp.logical_or(c == 1, whole))
    def _():
        e_copy().wait_recv()

    for j in range(4):

        def take():
            later[j] = landed[j].astype(F32).reshape(PIX, C).astype(BF16)

        if j < 2:
            take()
        else:
            pl.when(whole)(take)

            @pl.when(jnp.logical_not(whole))
            def _():
                later[j] = jnp.zeros((PIX, C), BF16)

    loads[1].wait()
    grad_act = jnp.zeros((PIX, C), F32)
    for k in range(3):
        grad_act = grad_act + lax.dot_general(
            later[c + k], w_time[C * k : C * k + C, :], CONTRACT_COLS, preferred_element_type=F32
        )
    grad_normed = grad_act.astype(BF16).astype(F32) * slope
    grad_hidden = (grad_normed - group_mean(grad_normed) - normed * group_mean(grad_normed * normed)) * inv_std
    grad_low = grad_hidden.astype(BF16)
    grads[c] = grad_low
    pair_copy(2, grads).start()

    for j in range(4):
        later_rows[j] = own_rows(later[j].astype(F32).T, c)
    pair_copy(1, acts).wait_recv()
    for k in range(3):
        time_part[:, C * k : C * k + C] = jnp.dot(
            later_rows[k], acts[0], preferred_element_type=F32
        ) + jnp.dot(later_rows[k + 1], acts[1], preferred_element_type=F32)

    parts = []
    for index in range(3):
        part = Part()
        part.order = ORDERS[index]
        if index < 2:
            (part.data, part.land_a, part.go_b, part.land_b, part.sum1, part.go2, part.got2, part.sum2, part.go3,
             part.got3, part.sems1, part.sems2, part.sems3) = part_refs[13 * index : 13 * index + 13]
        else:
            (part.data, part.got1, part.sum1, part.go2, part.got2, part.sum2, part.go3,
             part.got3, part.sems1, part.sems2, part.sems3) = part_refs[26:37]
        parts.append(part)
    ring_p, ring_q, direct = parts

    def hop(part, level, k):
        axis = part.order[level]
        sends = (part.data, part.go2, part.go3)[level]
        lands = (None if part is not direct else part.got1, part.got2, part.got3)[level]
        sems = (part.sems1, part.sems2, part.sems3)[level]
        goal = lax.rem(at[axis] + k, SIZES[axis])
        return copy(sends.at[goal], lands.at[k - 1], sems.at[0, k - 1], sems.at[1, k - 1], partner(axis, k))

    def ring_hop(part, stage, d):
        axis = part.order[0]
        goal = lax.rem(at[axis] + (1, 3)[d], 4)
        far = lax.rem(at[axis] + 2, 4)
        half = pl.ds(2 * d, 2)
        other = pl.ds(2 - 2 * d, 2)
        src, dst = (
            (part.data.at[far, half], part.land_a.at[d]),
            (part.data.at[goal, other], part.land_b.at[d, other]),
            (part.go_b.at[d], part.land_b.at[d, half]),
        )[stage]
        return copy(src, dst, part.sems1.at[0, stage, d], part.sems1.at[1, stage, d], partner(axis, (1, 3)[d]))

    def time_cols(i, start, size):
        return time_part[:, pl.ds(pl.multiple_of(384 * i + start, 128), size)].reshape(32, 8, size)

    for i in range(NX):
        rest = jnp.concatenate([time_cols(i, 0, 128), time_cols(i, 128, 128)], axis=1).astype(BF16)
        rest = rest.reshape(NY, NZ, 16, 128)
        for zz in range(NZ):
            direct.data[zz, :, i] = rest[:, zz]
    for k in range(1, NZ):
        hop(direct, 0, k).start()

    grad_rows[c] = own_rows(grads[c].astype(F32).T, c)
    pair_copy(2, grads).wait_recv()
    grad_rows[1 - c] = own_rows(grads[1 - c].astype(F32).T, c)

    def spatial(i, ch):
        n = 3 * i + ch
        a = n // 4
        top = pl.ds(pl.multiple_of(128 * a, 128), PIX)
        side = pl.ds(pl.multiple_of(384 * lax.rem(n, 4), 128), 384)
        total = jnp.dot(grad_rows[0], windows[0, top, side], preferred_element_type=F32) + jnp.dot(
            grad_rows[1], windows[1, top, side], preferred_element_type=F32
        )
        return total.reshape(32, 8, 384)

    for j in (2, 1, 3, 0):
        i = lax.rem(x + j, NX)
        s0, s1, s2 = [spatial(i, ch) for ch in range(3)]
        ring_p.data[i] = jnp.concatenate([s0, s1], axis=1).astype(BF16).reshape(NY, NZ, 16, 384)
        tail = jnp.concatenate([s2[:, :, 256:], time_cols(i, 256, 128)], axis=2)
        mixed = jnp.concatenate([s2[:, :, :256], tail], axis=1).astype(BF16).reshape(NY, NZ, 16, 256)
        for yy in range(NY):
            ring_q.data[yy, i] = mixed[yy]
        if j == 2:
            ring_hop(ring_p, 0, 0).start()
            ring_hop(ring_p, 0, 1).start()
        elif j == 1:
            ring_hop(ring_p, 1, 0).start()
        elif j == 3:
            ring_hop(ring_p, 1, 1).start()
    for stage in range(2):
        for d in range(2):
            ring_hop(ring_q, stage, d).start()

    fill(grad_windows, grads[c].astype(F32), grads[c], True)

    def backward(a):
        for b in range(3):
            tap = 3 * a + b
            part = lax.dot_general(
                grad_windows[128 * (2 - a) : 128 * (2 - a) + PIX, C * b : C * b + C],
                weights[C * tap : C * tap + C, :],
                CONTRACT_COLS,
                preferred_element_type=F32,
            )
            if tap == 0:
                acc[...] = part
            else:
                acc[...] += part

    def relay(part):
        axis = part.order[0]
        for d in range(2):
            goal = lax.rem(at[axis] + (1, 3)[d], 4)
            ring_hop(part, 0, d).wait_recv()
            part.go_b[d] = (
                part.data[goal, 2 * d : 2 * d + 2].astype(F32) + part.land_a[d].astype(F32)
            ).astype(BF16)
            ring_hop(part, 2, d).start()

    backward(0)
    relay(ring_p)
    relay(ring_q)
    backward(1)
    backward(2)
    gx_low[...] = acc[...].astype(BF16)
    gx_out = pltpu.make_async_copy(gx_low, gx_ref, local_sem.at[7])
    gx_out.start()

    def second(part, total):
        part.sum1[...] = total
        part.go2[...] = total.astype(BF16)
        for k in range(1, SIZES[part.order[1]]):
            hop(part, 1, k).start()

    def ring_total(part):
        for stage in (1, 2):
            for d in range(2):
                ring_hop(part, stage, d).wait_recv()
        mine = at[part.order[0]]
        return part.data[mine].astype(F32) + part.land_b[0].astype(F32) + part.land_b[1].astype(F32)

    second(ring_q, ring_total(ring_q))
    second(ring_p, ring_total(ring_p))
    total = direct.data[z].astype(F32)
    for k in range(1, NZ):
        hop(direct, 0, k).wait_recv()
        total = total + direct.got1[k - 1].astype(F32)
    second(direct, total)
    for part in (ring_q, ring_p, direct):
        total = part.sum1[at[part.order[1]]]
        for k in range(1, SIZES[part.order[1]]):
            hop(part, 1, k).wait_recv()
            total = total + part.got2[k - 1].astype(F32)
        part.sum2[...] = total
        part.go3[...] = total.astype(BF16)
        for k in range(1, SIZES[part.order[2]]):
            hop(part, 2, k).start()
    results = []
    for part in (ring_q, ring_p, direct):
        total = part.sum2[at[part.order[2]]]
        for k in range(1, SIZES[part.order[2]]):
            hop(part, 2, k).wait_recv()
            total = total + part.got3[k - 1].astype(F32)
        results.append(total * scale)
    mixed, first, last = results
    spatial_ref[:, 0:384] = first[0:8]
    spatial_ref[:, 384:768] = first[8:16]
    spatial_ref[:, 768:1024] = mixed[0:8]
    spatial_ref[:, 1024:1152] = mixed[8:16, 0:128]
    time_ref[:, 0:128] = last[0:8]
    time_ref[:, 128:256] = last[8:16]
    time_ref[:, 256:384] = mixed[8:16, 128:256]

    gx_out.wait()
    for j in range(1, NY):
        y_copy(j).wait_send()
    for piece in range(PIECES):
        w_copy(0, piece).wait_send()
        w_copy(1, piece).wait_send()
        f_copy(piece).wait_send()
        for index in range(3):
            s_copy(index, piece).wait_send()
    pair_copy(0, frames).wait_send()
    pair_copy(1, acts).wait_send()
    pair_copy(2, grads).wait_send()

    @pl.when(keeps)
    def _():
        e_copy().wait_send()

    for j in range(NY):

        def leave(k, carry):
            @pl.when(wanted(lax.rem(spot + k, 16)))
            def _():
                z_copy(j, k).wait_send()

            return carry

        lax.fori_loop(1, 16, leave, 0)
    for part in parts:
        if part is direct:
            for k in range(1, NZ):
                hop(part, 0, k).wait_send()
        else:
            for stage in range(3):
                for d in range(2):
                    ring_hop(part, stage, d).wait_send()
        for level in (1, 2):
            for k in range(1, SIZES[part.order[level]]):
                hop(part, level, k).wait_send()


def block_pass(frames, w_spatial, w_time, gain, bias, grad_out, scale):
    vmem = pl.BlockSpec(memory_space=pltpu.VMEM)
    anywhere = pl.BlockSpec(memory_space=pl.ANY)
    dma = pltpu.SemaphoreType.DMA
    scratch = [
        pltpu.VMEM((TAP_ROWS, C), BF16),
        pltpu.VMEM((3 * C, C), BF16),
        pltpu.VMEM((2, PIX, C), BF16),
        pltpu.VMEM((2, 768, 3 * C), BF16),
        pltpu.VMEM((768, 3 * C), BF16),
        pltpu.VMEM((4, NY, 16, 8, C), BF16),
        pltpu.VMEM((NY - 1, 16, 8, C), BF16),
        pltpu.VMEM((4, PIX, C), BF16),
        pltpu.VMEM((4, 256, PIX), BF16),
        pltpu.VMEM((2, PIX, C), BF16),
        pltpu.VMEM((2, PIX, C), BF16),
        pltpu.VMEM((2, 256, PIX), BF16),
        pltpu.VMEM((PIX, C), F32),
        pltpu.VMEM((256, 3 * C), F32),
        pltpu.VMEM((PIX, C), BF16),
        dma((2, PIECES)), dma((2, PIECES)), dma((PIECES,)), dma((PIECES,)), dma((3, PIECES)), dma((3, PIECES)),
        dma((NY - 1,)), dma((NY - 1,)), dma((NY, 15)), dma((NY, 15)), dma((2,)), dma((2, 3)), dma((8,)),
    ]
    for order, lanes in zip(ORDERS, LANES):
        n1, n2, n3 = [SIZES[axis] for axis in order]
        scratch.append(pltpu.VMEM((n1, n2, n3, 16, lanes), BF16))
        if n1 == 4:
            scratch += [
                pltpu.VMEM((2, 2, n3, 16, lanes), BF16),
                pltpu.VMEM((2, 2, n3, 16, lanes), BF16),
                pltpu.VMEM((2, 4, n3, 16, lanes), BF16),
            ]
        else:
            scratch.append(pltpu.VMEM((n1 - 1, n2, n3, 16, lanes), BF16))
        scratch += [
            pltpu.VMEM((n2, n3, 16, lanes), F32),
            pltpu.VMEM((n2, n3, 16, lanes), BF16),
            pltpu.VMEM((n2 - 1, n3, 16, lanes), BF16),
            pltpu.VMEM((n3, 16, lanes), F32),
            pltpu.VMEM((n3, 16, lanes), BF16),
            pltpu.VMEM((n3 - 1, 16, lanes), BF16),
            dma((2, 3, 2)) if n1 == 4 else dma((2, n1 - 1)),
            dma((2, n2 - 1)),
            dma((2, n3 - 1)),
        ]

    def kernel(*refs):
        block_kernel(scale, *refs)

    return pl.pallas_call(
        kernel,
        out_shape=(
            jax.ShapeDtypeStruct((PIX, C), BF16),
            jax.ShapeDtypeStruct((8, 1152), F32),
            jax.ShapeDtypeStruct((8, 384), F32),
        ),
        in_specs=[anywhere] * 3 + [vmem] * 2 + [anywhere],
        out_specs=(anywhere, vmem, vmem),
        scratch_shapes=scratch,
        compiler_params=pltpu.CompilerParams(
            collective_id=0, has_side_effects=True, vmem_limit_bytes=58 * 1024 * 1024
        ),
        name="block_pass",
    )(frames, w_spatial, w_time, gain, bias, grad_out)


def shards(clips, w_spatial, w_time, norm_gain, norm_bias, grad_out):
    scale = float(PIX * 64 * NX) ** (-0.5)
    grad_clips, spatial, time = block_pass(
        clips.reshape(PIX, C),
        w_spatial,
        w_time,
        norm_gain.reshape(1, C),
        norm_bias.reshape(1, C),
        grad_out.reshape(64, 8, C),
        scale,
    )
    return grad_clips.reshape(clips.shape), spatial.T, time.T


def solution(mesh):
    return jax.shard_map(
        shards,
        mesh=mesh,
        in_specs=(
            P("dp", "wide", None, None, None),
            P(None, "dp"),
            P(),
            P(),
            P(),
            P("dp", None, "wide", None),
        ),
        out_specs=(P("dp", "wide", None, None, None), P("dp", "wide"), P("dp", "wide")),
        check_vma=False,
    )
```

time: 498 us -> 81.5 us (0.16)
  waiting for transfers between devices: 354 us -> 0 us
  Pallas kernels: 0 us -> 75.3 us
  matrix products: 40.3 us -> 0 us
  local copies, waits for them, and re-layouts: 40.7 us -> 4.56 us
  blocking collectives: 23.4 us -> 0 us
  between operations: 14.2 us -> 0.64 us
  starting transfers between devices: 12.4 us -> 0 us
  other arithmetic: 11.7 us -> 0 us
    unnamed x7 -> x0, waiting for transfers between devices: 230 us -> none
    pallas_call x0 -> x1, Pallas kernels: none -> 75.3 us  [block_pass(): pl.pallas_call(kernel, out_shape=(jax.ShapeDtypeStruct((PIX, C), BF16), j...]
    reduce_scatter x2 -> x0, waiting for transfers between devices: 60.1 us -> none  [the longest x1 36.1 us: shards(): lax.psum_scatter(partial_pair[0], 'dp', scatter_dimension=0, tiled=True)]
    all_gather x1 -> x0, waiting for transfers between devices: 51.6 us -> none  [shards(): weights = lax.all_gather(w_spatial, 'dp', axis=1, tiled=True)]
    dot_general x33 -> x0, matrix products: 40.3 us -> none  [the longest x9 13.8 us: spatial_backward(): lax.dot_general(window, grad_flat, CONTRACT_ROWS, preferred_element_type=...]
    all_to_all x1 -> x0, blocking collectives: 23.4 us -> none  [shards(): lax.all_to_all(grad_act, 'wide', split_axis=1, concat_axis=2, tiled=True)]
    unnamed x31 -> x3, local copies, waits for them, and re-layouts: 27.6 us -> 4.56 us
    all_to_all x1 -> x0, waiting for transfers between devices: 12.3 us -> none  [shards(): tiles = lax.all_to_all(act, 'wide', split_axis=2, concat_axis=1, tiled=True)]
  transfers between devices with their start and end apart: 6 -> 0, of which waited for: 6 -> 0; matrix products, arithmetic and copies ran while one was open for 12% -> 0% of each run, Pallas kernels for 0% -> 0%
where the time goes in v2:
time: 81.5 us; the launch traced here: 80.5 us
  Pallas kernels  75.3 us (92%)
  local copies, waits for them, and re-layouts  4.56 us (6%)
    pallas_call x1, Pallas kernels, block_pass(): pl.pallas_call(kernel, out_shape=(jax.ShapeDtypeStruct((PIX, C), BF16), j...  75.3 us
    unnamed x3, local copies, waits for them, and re-layouts  4.56 us

profile of v2, /device:TPU:1, one launch (start us, length us, event | category | flops | bytes accessed | tf_op | source)
XLA Modules:
  0.0 80.5 jit_solution(3574855566903463228)
XLA Ops:
  0.6 75.3 %block_pass.1 = (bf16[512,512]{1,0:T(8,128)(2,1)}, f32[8,1152]{1,0:T(8,128)}, f32[8,384]{1,0:T(8,128)}) custom-call(bf16[512,512]{1,0:T(8,128)(2,1)} %bitcast.8, bf16[4608,128]{1,0:T(8,128)(2,1)} %refs_1_.1, bf16[1536,512]{1,0:T(8,128)(2,1)} %refs_2_.1, f32[1,512]{1,0:T(1,128)} %bitcast.12, f32[1,512]{1,0:T(1,128)} %bitcast.13, bf16[64,8,512]{2,1,0:T(8,128)(2,1)} %bitcast.9), custom_call_target="tpu_custom_call" | custom-call | tf_op jit(solution)/shard_map/block_pass/pallas_call | solution.py:562
  75.9 1.9 %copy.12 = bf16[1,1,4,128,512]{4,3,2,1,0:T(8,128)(2,1)} copy(bf16[1,1,4,128,512]{4,3,2,1,0:T(8,128)(2,1)} %bitcast.7) | data formatting | bytes 1048576
  77.8 1.4 %copy.13 = f32[1152,8]{0,1:T(8,128)} copy(f32[1152,8]{0,1:T(8,128)} %bitcast.10) | data formatting | bytes 73728
  79.2 1.3 %copy.14 = f32[384,8]{0,1:T(8,128)} copy(f32[384,8]{0,1:T(8,128)} %bitcast.11) | data formatting | bytes 24576
